TPU v7x, 32 devices: a whole 2x2x4 slice. The times are simulated.
32 devices in a mesh: pool: 2 (over x), pencil: 8 (over z, y), tgroup: 2 (over core).
Axes of the slice: x: 2, y: 2, z: 4, core: 2. Of those that a mesh axis runs over, the one named last changes fastest.
Arguments:
- dpsi: float32 [2, 4, 196608], P(None, 'pool', ('pencil', 'tgroup')), parts along dimension 1, may hold values from -6 to 6
- stick_cols: int32 [3072], replicated, may hold values from 0 to 16383, as said below
- pw_z: int32 [3072, 64], P('pencil'), may hold values from 0 to 127, as said below
- v_local: float32 [128, 16384], P('pencil'), may hold values from -6 to 6
- dv: float32 [128, 16384], P('pencil'), may hold values from -6 to 6
Outputs:
- h_dpsi: float32 [2, 4, 196608], P(None, 'pool', ('pencil', 'tgroup')), parts along dimension 1
There are 2 independent parts, one for each index of `pool`. A program takes and returns all parts, laid end to end along the dimension named above; an argument that names none is the same for every part. Nothing has to cross between parts.
Inputs may be any that keep to these rules, and one draw needn't show every extreme that they name: `stick_cols`: the 3072 values are distinct. `pw_z`: the 64 values of each row are distinct.
All inputs are finite; a program needn't handle non-finite values.
Results may differ from a plain program's by a relative error of at most 0.00007.
Values sent between devices are 32-bit elements; how exact they have to be, the bound alone decides.
A program may use at most 128 MiB of HBM per device.

v0:
```python
from functools import partial
import math

import jax
import jax.numpy as jnp
import ml_dtypes
import numpy as np
from jax import lax
from jax.experimental import pallas as pl
from jax.experimental.pallas import tpu as pltpu
from jax.sharding import PartitionSpec as P

F32 = jnp.float32
BF16 = jnp.bfloat16
LANES = 128
GROUP = 8


def halves(table):
    hi = table.astype(ml_dtypes.bfloat16)
    lo = (table - hi.astype(np.float64)).astype(ml_dtypes.bfloat16)
    return jnp.asarray(hi), jnp.asarray(lo)


def split(value):
    hi = value.astype(BF16)
    lo = (value - hi.astype(F32)).astype(BF16)
    return hi, lo


def dot3(left, right, dims=((1,), (0,))):
    mul = lambda a, b: lax.dot_general(a, b, (dims, ((), ())), preferred_element_type=F32)
    return mul(left[0], right[0]) + (mul(left[0], right[1]) + mul(left[1], right[0]))


def waves(length):
    k = np.arange(length)
    angle = (k[:, None] * k[None, :] % length) * (2.0 * math.pi / length)
    return np.cos(angle) / math.sqrt(length), np.sin(angle) / math.sqrt(length)


def depth_table(length, devices):
    cos, sin = waves(length)
    planes = length // devices
    whole = np.stack([np.stack([cos, -sin], 1), np.stack([sin, cos], 1)])
    whole = whole.reshape(2, devices, planes, 2 * length)
    return whole.transpose(1, 0, 2, 3).reshape(2 * length, 2 * length)


def row_tables(length):
    cos, sin = waves(length)
    return np.concatenate([cos, sin]), np.concatenate([cos, -sin])


def column_table(length, slots):
    cos, sin = waves(length)
    whole = np.stack([np.stack([cos, -sin], 1), np.stack([sin, cos], 1)])
    whole = whole.reshape(2, length, 2, slots, length // slots)
    return whole.transpose(0, 1, 4, 2, 3).reshape(2 * length, 2 * length)


class Peers:
    def __init__(self):
        self.cores = lax.axis_size("tgroup")
        self.count = lax.axis_size("pencil") * self.cores
        self.me = lax.axis_index("pencil") * self.cores + lax.axis_index("tgroup")
        self.barrier = pltpu.get_barrier_semaphore()

    def at(self, step):
        return lax.rem(self.me + step, self.count)

    def name(self, device):
        return {"pencil": lax.div(device, self.cores), "tgroup": lax.rem(device, self.cores)}

    def greet(self):
        @pl.loop(1, self.count)
        def _(step):
            pl.semaphore_signal(
                self.barrier,
                inc=1,
                device_id=self.name(self.at(step)),
                device_id_type=pl.DeviceIdType.MESH,
            )

    def met(self):
        pl.semaphore_wait(self.barrier, self.count - 1)

    def copy(self, step, source, target, sent, got):
        peer = self.at(step)
        return pltpu.make_async_remote_copy(
            src_ref=source.at[peer],
            dst_ref=target.at[self.me],
            send_sem=sent.at[step],
            recv_sem=got.at[step],
            device_id=self.name(peer),
            device_id_type=pl.DeviceIdType.MESH,
        )

    def settle(self, source, target, sent, got):
        @pl.loop(1, self.count)
        def _(step):
            self.copy(step, source, target, sent, got).wait()


def depth_up(
    coeff_ref,
    pw_ref,
    table_hi,
    table_lo,
    local_ref,
    change_ref,
    out_ref,
    weight_ref,
    ready,
    first,
    second,
    sent,
    got,
    loads,
):
    peers = Peers()
    peers.greet()
    fetch = [
        pltpu.make_async_copy(local_ref, first, loads.at[0]),
        pltpu.make_async_copy(change_ref, second, loads.at[1]),
    ]
    for copy in fetch:
        copy.start()
    _, bands, rows, width = coeff_ref.shape
    devices, part_rows, _ = out_ref.shape
    zpw = width // 2
    pw = pw_ref[...]
    z = lax.broadcasted_iota(jnp.int32, (rows, LANES), 1)
    pieces = [[None] * 2 for _ in range(bands)]
    for parity in range(2):
        source = jnp.full((rows, LANES), -1, jnp.int32)
        for k in range(parity * zpw, (parity + 1) * zpw):
            source = jnp.where(pw[:, k : k + 1] == z, k, source)
        found = source >= 0
        source = jnp.maximum(source, 0)
        for band in range(bands):
            parts = []
            for part in range(2):
                taken = jnp.take_along_axis(
                    coeff_ref[part, band], source, axis=1, mode="promise_in_bounds"
                )
                parts.append(jnp.where(found, taken, 0.0))
            pieces[band][parity] = jnp.concatenate(parts, axis=1)
    column = jnp.concatenate([piece for pair in pieces for piece in pair], axis=0)
    field = dot3((table_hi[...], table_lo[...]), split(column), ((1,), (1,)))
    for device in range(devices):
        ready[device] = field[device * part_rows : (device + 1) * part_rows]
    peers.met()

    @pl.loop(1, devices)
    def _(step):
        peers.copy(step, ready, out_ref, sent, got).start()

    out_ref[peers.me] = ready[peers.me]
    for copy in fetch:
        copy.wait()
    planes = part_rows // 2
    core = lax.axis_index("tgroup")
    for x in range(weight_ref.shape[0] // planes):
        lanes = slice(x * LANES, (x + 1) * LANES)
        whole = first[:, lanes] + second[:, lanes]
        mine = whole[:planes]
        for other in range(1, peers.cores):
            mine = jnp.where(core == other, whole[other * planes : (other + 1) * planes], mine)
        weight_ref[x * planes : (x + 1) * planes] = mine
    peers.settle(ready, out_ref, sent, got)


def turn(value):
    half = value.shape[0] // 2
    return jnp.concatenate([-value[half:], value[:half]], axis=0)


def plane_kernel(
    bands,
    cols_ref,
    field_ref,
    weight_ref,
    up_hi,
    up_lo,
    down_hi,
    down_lo,
    column_hi,
    column_lo,
    back_hi,
    back_lo,
    grid,
    flat,
    sticks,
):
    devices, part_rows, block = field_ref.shape
    planes = part_rows // 2
    own = block // bands
    pairs = own // 2
    length = weight_ref.shape[1]
    bz = bands * planes
    slots = LANES // (2 * bz)
    inner = length // slots
    group_rows = inner * length
    batch = math.gcd(inner, 4)
    total = devices * own
    shift = group_rows.bit_length() - 1

    grid[...] = jnp.zeros_like(grid)
    for device in range(devices):
        for part in range(2):
            for band in range(bands):
                flat[
                    (part * bands + band) * planes : (part * bands + band + 1) * planes,
                    device * own : (device + 1) * own,
                ] = field_ref[
                    device, part * planes : (part + 1) * planes, band * own : (band + 1) * own
                ]
    for tile in range(total // LANES):
        value = flat[:, tile * LANES : (tile + 1) * LANES]
        value = jnp.concatenate([value[:bz]] * slots + [value[bz:]] * slots, axis=0)
        sticks[tile * LANES : (tile + 1) * LANES] = value.T

    lane = lax.broadcasted_iota(jnp.int32, (1, LANES), 1)
    slot_of_lane = lane // bz % slots
    chunks = pairs // GROUP

    @pl.loop(0, devices * chunks)
    def _(step):
        device = lax.div(step, chunks)
        start = (step - device * chunks) * GROUP
        first = device * own + 2 * start
        cols = [cols_ref[first + i] for i in range(2 * GROUP)]
        rows = [col & (group_rows - 1) for col in cols]
        masks = [slot_of_lane == lax.shift_right_logical(col, shift) for col in cols]
        base = pl.multiple_of(device * own + start, GROUP)
        places = [base + (i % 2) * pairs + i // 2 for i in range(2 * GROUP)]
        values = [sticks[pl.ds(place, 1), :] for place in places]
        for value, row, mask in zip(values, rows, masks):
            pltpu.store(grid.at[pl.ds(row, 1), :], value, mask=mask)

    @pl.loop(0, inner // batch)
    def _(step):
        whole = pl.ds(pl.multiple_of(step * batch * length, batch * length), batch * length)
        his, los = [], []
        for i in range(batch):
            start = pl.multiple_of((step * batch + i) * length, length)
            hi, lo = split(grid[pl.ds(start, length), :].T)
            his.append(jnp.concatenate([hi, turn(hi)], axis=1))
            los.append(jnp.concatenate([lo, turn(lo)], axis=1))
        pair = (jnp.concatenate(his, axis=0), jnp.concatenate(los, axis=0))
        grid[whole, :] = dot3(pair, (up_hi[...], up_lo[...]))

    for z in range(planes):
        picks = [pl.ds(band * planes + z, 2 * length, stride=bz) for band in range(bands)]
        value = jnp.concatenate([grid[pick, :] for pick in picks], axis=1)
        value = dot3((column_hi[...], column_lo[...]), split(value))
        weight = weight_ref[pl.ds(z, length, stride=planes), :]
        weight = jnp.concatenate([weight] * 2, axis=0)
        weight = jnp.concatenate([weight] * bands, axis=1)
        value = dot3((back_hi[...], back_lo[...]), split(value * weight))
        for band, pick in enumerate(picks):
            grid[pick, :] = value[:, band * length : (band + 1) * length]

    @pl.loop(0, inner // batch)
    def _(step):
        his, los = [], []
        starts = [pl.multiple_of((step * batch + i) * length, length) for i in range(batch)]
        for start in starts:
            hi, lo = split(grid[pl.ds(start, length), :])
            his.append(jnp.concatenate([hi, turn(hi)], axis=1))
            los.append(jnp.concatenate([lo, turn(lo)], axis=1))
        pair = (jnp.concatenate(his, axis=0), jnp.concatenate(los, axis=0))
        value = dot3(pair, (down_hi[...], down_lo[...]))
        for i, start in enumerate(starts):
            grid[pl.ds(start, length), :] = value[i * length : (i + 1) * length].T


def depth_down(
    cols_ref,
    grid_ref,
    pw_ref,
    table_hi,
    table_lo,
    out_ref,
    ready,
    field,
    sticks,
    flat,
    sent,
    got,
):
    peers = Peers()
    peers.greet()
    _, bands, rows, width = out_ref.shape
    devices, part_rows, _ = ready.shape
    planes = part_rows // 2
    own = 2 * rows
    length = devices * planes
    bz = bands * planes
    slots = LANES // (2 * bz)
    half = slots * bz
    group_rows = grid_ref.shape[0]
    shift = group_rows.bit_length() - 1
    lane = lax.broadcasted_iota(jnp.int32, (1, LANES), 1)
    slot_of_lane = lane // bz % slots

    def gather(device):
        @pl.loop(0, rows // GROUP)
        def _(chunk):
            start = pl.multiple_of(chunk * GROUP, GROUP)
            first = device * own + 2 * start
            cols = [cols_ref[first + i] for i in range(2 * GROUP)]
            masks = [slot_of_lane == lax.shift_right_logical(col, shift) for col in cols]
            values = [grid_ref[pl.ds(col & (group_rows - 1), 1), :] for col in cols]
            for i, (value, mask) in enumerate(zip(values, masks)):
                sticks[pl.ds(start + (i % 2) * rows + i // 2, 1), :] = jnp.where(
                    mask, value, 0.0
                )

        tiles = []
        for tile in range(sticks.shape[0] // LANES):
            value = sticks[tile * LANES : (tile + 1) * LANES].T
            sums = []
            for part in range(2):
                terms = [
                    value[part * half + slot * bz : part * half + (slot + 1) * bz]
                    for slot in range(slots)
                ]
                sums.append(sum(terms[1:], terms[0]))
            tiles.append(jnp.concatenate(sums, axis=0))
        value = jnp.concatenate(tiles, axis=1)[:, :own]
        for part in range(2):
            for band in range(bands):
                start = (part * bands + band) * planes
                ready[
                    device, part * planes : (part + 1) * planes, band * own : (band + 1) * own
                ] = value[start : start + planes]

    sticks[...] = jnp.zeros_like(sticks)
    gather(peers.me)
    field[peers.me] = ready[peers.me]
    peers.met()

    @pl.loop(1, devices)
    def _(step):
        gather(peers.at(step))
        peers.copy(step, ready, field, sent, got).start()

    pw = pw_ref[...]
    first = lax.broadcasted_iota(jnp.int32, (rows, LANES), 1) < width // 2
    peers.settle(ready, field, sent, got)
    for device in range(devices):
        flat[device * part_rows : (device + 1) * part_rows] = field[device]
    column = dot3(split(flat[...]), (table_hi[...], table_lo[...]), ((0,), (0,)))
    for band in range(bands):
        for part in range(2):
            taken = []
            for parity in range(2):
                start = (band * 2 + parity) * rows
                piece = column[start : start + rows, part * length : (part + 1) * length]
                taken.append(
                    jnp.take_along_axis(piece, pw, axis=1, mode="promise_in_bounds")
                )
            out_ref[part, band] = jnp.where(first, taken[0], taken[1])


VM = pl.BlockSpec(memory_space=pltpu.VMEM)
SM = pl.BlockSpec(memory_space=pltpu.SMEM)
params = partial(pltpu.CompilerParams, vmem_limit_bytes=40 * 1024 * 1024)


def local(dpsi, stick_cols, pw_z, v_local, dv):
    devices = lax.axis_size("pencil") * lax.axis_size("tgroup")
    cores = lax.axis_size("tgroup")
    core = lax.axis_index("tgroup")
    length = math.isqrt(v_local.shape[1])
    planes = v_local.shape[0] // cores
    own = pw_z.shape[0] // cores
    zpw = pw_z.shape[1]
    bands = dpsi.shape[1]
    pairs = own // 2
    bz = bands * planes
    slots = LANES // (2 * bz)

    rows = lax.dynamic_slice_in_dim(pw_z, core * own, own, 0).reshape(pairs, 2 * zpw)
    coeff = dpsi.reshape(2, bands, pairs, 2 * zpw)

    depth = halves(depth_table(length, devices))
    up, down = [halves(table) for table in row_tables(length)]
    column = column_table(length, slots)
    back = halves(np.ascontiguousarray(column.T))
    column = halves(column)

    block = (devices, 2 * planes, bands * own)
    in_slots = length // slots * length
    padded = -(-own // LANES) * LANES
    field, potential = pl.pallas_call(
        depth_up,
        out_shape=[
            jax.ShapeDtypeStruct(block, F32),
            jax.ShapeDtypeStruct((length * planes, length), F32),
        ],
        in_specs=[VM] * 4 + [pl.BlockSpec(memory_space=pl.ANY)] * 2,
        out_specs=[VM, VM],
        scratch_shapes=[
            pltpu.VMEM(block, F32),
            pltpu.VMEM(v_local.shape, F32),
            pltpu.VMEM(v_local.shape, F32),
            pltpu.SemaphoreType.DMA((devices,)),
            pltpu.SemaphoreType.DMA((devices,)),
            pltpu.SemaphoreType.DMA((2,)),
        ],
        compiler_params=params(collective_id=0, has_side_effects=True),
    )(coeff, rows, *depth, v_local, dv)
    grid = pl.pallas_call(
        partial(plane_kernel, bands),
        out_shape=jax.ShapeDtypeStruct((in_slots, LANES), F32),
        in_specs=[SM] + [VM] * 10,
        out_specs=VM,
        scratch_shapes=[
            pltpu.VMEM((2 * bz, devices * own), F32),
            pltpu.VMEM((devices * own, LANES), F32),
        ],
        compiler_params=params(),
    )(stick_cols, field, potential, *up, *down, *column, *back)
    output = pl.pallas_call(
        depth_down,
        out_shape=jax.ShapeDtypeStruct(coeff.shape, F32),
        in_specs=[SM] + [VM] * 4,
        out_specs=VM,
        scratch_shapes=[
            pltpu.VMEM(block, F32),
            pltpu.VMEM(block, F32),
            pltpu.VMEM((padded, LANES), F32),
            pltpu.VMEM((2 * length, bands * own), F32),
            pltpu.SemaphoreType.DMA((devices,)),
            pltpu.SemaphoreType.DMA((devices,)),
        ],
        compiler_params=params(collective_id=1, has_side_effects=True),
    )(stick_cols, grid, rows, *depth)
    return output.reshape(dpsi.shape)


def solution(mesh):
    in_specs = (
        P(None, "pool", ("pencil", "tgroup")),
        P(),
        P("pencil", None),
        P("pencil", None),
        P("pencil", None),
    )
    out_specs = P(None, "pool", ("pencil", "tgroup"))
    return jax.shard_map(local, mesh=mesh, in_specs=in_specs, out_specs=out_specs, check_vma=False)
```

profile of v0, /device:TPU:0, one launch (start us, length us, event | category | flops | bytes accessed | tf_op | source)
XLA Modules:
  0.0 56.0 jit_solution(18169156008598074630)
XLA Ops:
  0.0 0.0 copy-start
  0.0 0.0 copy-start.10
  0.0 0.0 copy-start.11
  0.0 0.0 copy-start.12
  0.1 0.0 copy-start.13
  0.1 0.0 copy-start.14
  0.1 0.8 %copy-done = s32[384,64]{0,1:T(8,128)S(1)} copy-done((s32[384,64]{0,1:T(8,128)S(1)}, s32[384,64]{0,1:T(8,128)}, u32[]{:S(2)}) %copy-start) | copy-done | bytes 98328
  0.9 0.1 constant_dynamic-slice_fusion
  1.0 0.1 copy.17
  1.1 0.1 reshape.10.pw_ref
  1.2 1.1 %reshape.9.coeff_ref = f32[2,2,96,128]{3,2,1,0:T(8,128)S(1)} reshape(f32[2,2,12288]{2,1,0:T(2,128)} %param.15) | data formatting | bytes 393216 | tf_op jit(solution)/shard_map/reshape | solution.py:387
  2.3 0.0 copy-start.1
  2.3 1.2 %copy-done.1 = f32[16,16384]{1,0:T(8,128)S(1)} copy-done((f32[16,16384]{1,0:T(8,128)S(1)}, f32[16,16384]{1,0:T(8,128)}, u32[]{:S(2)}) %copy-start.1) | copy-done | bytes 1048600
  3.5 1.2 %copy-done.2 = f32[16,16384]{1,0:T(8,128)S(1)} copy-done((f32[16,16384]{1,0:T(8,128)S(1)}, f32[16,16384]{1,0:T(8,128)}, u32[]{:S(2)}) %copy-start.2) | copy-done | bytes 1048600
  4.7 0.9 %copy-done.3 = bf16[256,256]{1,0:T(8,128)(2,1)S(1)} copy-done((bf16[256,256]{1,0:T(8,128)(2,1)S(1)}, bf16[256,256]{1,0:T(8,128)(2,1)}, u32[]{:S(2)}) %copy-start.3) | copy-done | bytes 131096
  5.6 0.9 %copy-done.5 = bf16[256,256]{1,0:T(8,128)(2,1)S(1)} copy-done((bf16[256,256]{1,0:T(8,128)(2,1)S(1)}, bf16[256,256]{1,0:T(8,128)(2,1)}, u32[]{:S(2)}) %copy-start.5) | copy-done | bytes 131096
  6.5 14.0 %shard_map.145 = (f32[16,16,384]{2,1,0:T(8,128)S(1)}, f32[1024,128]{1,0:T(8,128)S(1)}) custom-call(f32[2,2,96,128]{3,2,1,0:T(8,128)S(1)} %reshape.9.coeff_ref, s32[96,128]{1,0:T(8,128)S(1)} %reshape.10.pw_ref, bf16[256,256]{1,0:T(8,128)(2,1)S(1)} %copy-done.5, bf16[256,256]{1,0:T(8,128)(2,1)S(1)} %copy-done.3, f32[16,16384]{1,0:T(8,128)S(1)} %copy-done.1, ...), custom_call_target="tpu_custom_call" | custom-call | tf_op jit(solution)/shard_map/pallas_call | solution.py:398
  20.6 0.0 copy-start.4
  20.6 0.0 copy-start.6
  20.7 17.3 %shard_map.146.grid_ref = f32[4096,128]{1,0:T(8,128)S(1)} custom-call(s32[3072]{0:T(1024)S(1)} %copy-done.15, f32[16,16,384]{2,1,0:T(8,128)S(1)} %get-tuple-element.7.field_ref, f32[1024,128]{1,0:T(8,128)S(1)} %get-tuple-element.8.weight_ref, bf16[256,128]{1,0:T(8,128)(2,1)S(1)} %copy-done.14, bf16[256,128]{1,0:T(8,128)(2,1)S(1)} %copy-done.13, ...), custom_call_target="tpu_custom_call" | custom-call | tf_op jit(solution)/shard_map/pallas_call | solution.py:416
  38.0 0.0 copy-done.4
  38.0 0.0 copy-done.6
  38.0 17.2 %shard_map.147 = f32[2,2,96,128]{3,2,1,0:T(8,128)S(1)} custom-call(s32[3072]{0:T(1024)S(1)} %copy-done.15, f32[4096,128]{1,0:T(8,128)S(1)} %shard_map.146.grid_ref, s32[96,128]{1,0:T(8,128)S(1)} %reshape.10.pw_ref, bf16[256,256]{1,0:T(8,128)(2,1)S(1)} %copy-done.6, bf16[256,256]{1,0:T(8,128)(2,1)S(1)} %copy-done.4), custom_call_target="tpu_custom_call" | custom-call | tf_op jit(solution)/shard_map/pallas_call | solution.py:427
  55.2 0.8 %reshape.11 = f32[2,2,12288]{2,1,0:T(2,128)} reshape(f32[2,2,96,128]{3,2,1,0:T(8,128)S(1)} %shard_map.147) | data formatting | bytes 393216 | tf_op jit(solution)/shard_map/reshape | solution.py:442
  (16 shorter events, 0.0 us)
Async XLA Ops:
  0.0 0.9 %copy-start = (s32[384,64]{0,1:T(8,128)S(1)}, s32[384,64]{0,1:T(8,128)}, u32[]{:S(2)}) copy-start(s32[384,64]{0,1:T(8,128)} %param.17) | copy-start | bytes 294916
  0.0 20.6 %copy-start.7 = (bf16[256,256]{1,0:T(8,128)(2,1)S(1)}, bf16[256,256]{1,0:T(8,128)(2,1)}, u32[]{:S(2)}) copy-start(bf16[256,256]{1,0:T(8,128)(2,1)} %constant.39.clone.column_lo) | copy-start | bytes 393220
  0.0 20.6 %copy-start.8 = (bf16[256,256]{1,0:T(8,128)(2,1)S(1)}, bf16[256,256]{1,0:T(8,128)(2,1)}, u32[]{:S(2)}) copy-start(bf16[256,256]{1,0:T(8,128)(2,1)} %constant.38.clone.column_hi) | copy-start | bytes 393220
  0.0 20.6 %copy-start.9 = (bf16[256,256]{1,0:T(8,128)(2,1)S(1)}, bf16[256,256]{1,0:T(8,128)(2,1)}, u32[]{:S(2)}) copy-start(bf16[256,256]{1,0:T(8,128)(2,1)} %constant.37.clone.back_lo) | copy-start | bytes 393220
  0.0 20.6 %copy-start.10 = (bf16[256,256]{1,0:T(8,128)(2,1)S(1)}, bf16[256,256]{1,0:T(8,128)(2,1)}, u32[]{:S(2)}) copy-start(bf16[256,256]{1,0:T(8,128)(2,1)} %constant.36.clone.back_hi) | copy-start | bytes 393220
  0.0 20.6 %copy-start.11 = (bf16[256,128]{1,0:T(8,128)(2,1)S(1)}, bf16[256,128]{1,0:T(8,128)(2,1)}, u32[]{:S(2)}) copy-start(bf16[256,128]{1,0:T(8,128)(2,1)} %constant.35.clone.down_lo) | copy-start | bytes 196612
  0.0 20.6 %copy-start.12 = (bf16[256,128]{1,0:T(8,128)(2,1)S(1)}, bf16[256,128]{1,0:T(8,128)(2,1)}, u32[]{:S(2)}) copy-start(bf16[256,128]{1,0:T(8,128)(2,1)} %constant.34.clone.down_hi) | copy-start | bytes 196612
  0.1 20.6 %copy-start.13 = (bf16[256,128]{1,0:T(8,128)(2,1)S(1)}, bf16[256,128]{1,0:T(8,128)(2,1)}, u32[]{:S(2)}) copy-start(bf16[256,128]{1,0:T(8,128)(2,1)} %constant.33.clone.up_lo) | copy-start | bytes 196612
  0.1 20.6 %copy-start.14 = (bf16[256,128]{1,0:T(8,128)(2,1)S(1)}, bf16[256,128]{1,0:T(8,128)(2,1)}, u32[]{:S(2)}) copy-start(bf16[256,128]{1,0:T(8,128)(2,1)} %constant.32.clone.up_hi) | copy-start | bytes 196612
  0.1 20.6 %copy-start.15 = (s32[3072]{0:T(1024)S(1)}, s32[3072]{0:T(1024)}, u32[]{:S(2)}) copy-start(s32[3072]{0:T(1024)} %cols_ref.3) | copy-start | bytes 36868
  2.3 1.2 %copy-start.1 = (f32[16,16384]{1,0:T(8,128)S(1)}, f32[16,16384]{1,0:T(8,128)}, u32[]{:S(2)}) copy-start(f32[16,16384]{1,0:T(8,128)} %local_ref.1) | copy-start | bytes 3145732
  3.5 1.2 %copy-start.2 = (f32[16,16384]{1,0:T(8,128)S(1)}, f32[16,16384]{1,0:T(8,128)}, u32[]{:S(2)}) copy-start(f32[16,16384]{1,0:T(8,128)} %change_ref.1) | copy-start | bytes 3145732
  4.7 0.9 %copy-start.3 = (bf16[256,256]{1,0:T(8,128)(2,1)S(1)}, bf16[256,256]{1,0:T(8,128)(2,1)}, u32[]{:S(2)}) copy-start(bf16[256,256]{1,0:T(8,128)(2,1)} %constant.31.clone.table_lo) | copy-start | bytes 393220
  5.6 0.9 %copy-start.5 = (bf16[256,256]{1,0:T(8,128)(2,1)S(1)}, bf16[256,256]{1,0:T(8,128)(2,1)}, u32[]{:S(2)}) copy-start(bf16[256,256]{1,0:T(8,128)(2,1)} %constant.30.clone.table_hi) | copy-start | bytes 393220
  20.6 17.4 %copy-start.4 = (bf16[256,256]{1,0:T(8,128)(2,1)S(1)}, bf16[256,256]{1,0:T(8,128)(2,1)}, u32[]{:S(2)}) copy-start(bf16[256,256]{1,0:T(8,128)(2,1)} %constant.31.clone.table_lo) | copy-start | bytes 393220
  20.6 17.4 %copy-start.6 = (bf16[256,256]{1,0:T(8,128)(2,1)S(1)}, bf16[256,256]{1,0:T(8,128)(2,1)}, u32[]{:S(2)}) copy-start(bf16[256,256]{1,0:T(8,128)(2,1)} %constant.30.clone.table_hi) | copy-start | bytes 393220
where the time goes:
time: 56.3 us; the launch traced here: 56 us
  Pallas kernels  48.5 us (86%)
  local copies, waits for them, and re-layouts  7.27 us (13%)
    pallas_call x1, Pallas kernels, local(): pl.pallas_call(partial(plane_kernel, bands), out_shape=jax.ShapeDtypeStru...  17.3 us
    pallas_call x1, Pallas kernels, local(): pl.pallas_call(depth_down, out_shape=jax.ShapeDtypeStruct(coeff.shape, F3...  17.2 us
    pallas_call x1, Pallas kernels, local(): pl.pallas_call(depth_up, out_shape=[jax.ShapeDtypeStruct(block, F32), jax...  14 us
    unnamed x32, local copies, waits for them, and re-layouts  5.12 us

commit v1 on v0

--- a/solution.py
+++ b/solution.py
@@ -13,7 +13,7 @@
 F32 = jnp.float32
 BF16 = jnp.bfloat16
 LANES = 128
-GROUP = 8
+GROUP = 32
 
 
 def halves(table):
@@ -68,6 +68,10 @@
 
     def at(self, step):
         return lax.rem(self.me + step, self.count)
+
+    def step(self, turn):
+        away = lax.div(turn, 2)
+        return self.count // 2 + jnp.where(lax.rem(turn, 2) == 0, away, -away)
 
     def name(self, device):
         return {"pencil": lax.div(device, self.cores), "tgroup": lax.rem(device, self.cores)}
@@ -105,13 +109,16 @@
 def depth_up(
     coeff_ref,
     pw_ref,
-    table_hi,
-    table_lo,
+    hi_ref,
+    lo_ref,
     local_ref,
     change_ref,
     out_ref,
     weight_ref,
     ready,
+    column,
+    table_hi,
+    table_lo,
     first,
     second,
     sent,
@@ -120,10 +127,8 @@
 ):
     peers = Peers()
     peers.greet()
-    fetch = [
-        pltpu.make_async_copy(local_ref, first, loads.at[0]),
-        pltpu.make_async_copy(change_ref, second, loads.at[1]),
-    ]
+    pairs = zip((hi_ref, lo_ref, local_ref, change_ref), (table_hi, table_lo, first, second))
+    fetch = [pltpu.make_async_copy(*pair, loads.at[i]) for i, pair in enumerate(pairs)]
     for copy in fetch:
         copy.start()
     _, bands, rows, width = coeff_ref.shape
@@ -131,7 +136,6 @@
     zpw = width // 2
     pw = pw_ref[...]
     z = lax.broadcasted_iota(jnp.int32, (rows, LANES), 1)
-    pieces = [[None] * 2 for _ in range(bands)]
     for parity in range(2):
         source = jnp.full((rows, LANES), -1, jnp.int32)
         for k in range(parity * zpw, (parity + 1) * zpw):
@@ -139,26 +143,27 @@
         found = source >= 0
         source = jnp.maximum(source, 0)
         for band in range(bands):
-            parts = []
+            places = pl.ds(band * 2 * rows + parity, rows, stride=2)
             for part in range(2):
                 taken = jnp.take_along_axis(
                     coeff_ref[part, band], source, axis=1, mode="promise_in_bounds"
                 )
-                parts.append(jnp.where(found, taken, 0.0))
-            pieces[band][parity] = jnp.concatenate(parts, axis=1)
-    column = jnp.concatenate([piece for pair in pieces for piece in pair], axis=0)
-    field = dot3((table_hi[...], table_lo[...]), split(column), ((1,), (1,)))
+                column[part, places, :] = jnp.where(found, taken, 0.0)
+    fetch[0].wait()
+    fetch[1].wait()
+    value = jnp.concatenate([column[0], column[1]], axis=1)
+    field = dot3((table_hi[...], table_lo[...]), split(value), ((1,), (1,)))
     for device in range(devices):
         ready[device] = field[device * part_rows : (device + 1) * part_rows]
     peers.met()
 
     @pl.loop(1, devices)
-    def _(step):
-        peers.copy(step, ready, out_ref, sent, got).start()
+    def _(turn):
+        peers.copy(peers.step(turn), ready, out_ref, sent, got).start()
 
     out_ref[peers.me] = ready[peers.me]
-    for copy in fetch:
-        copy.wait()
+    fetch[2].wait()
+    fetch[3].wait()
     planes = part_rows // 2
     core = lax.axis_index("tgroup")
     for x in range(weight_ref.shape[0] // planes):
@@ -176,33 +181,39 @@
     return jnp.concatenate([-value[half:], value[:half]], axis=0)
 
 
+def row_product(pair, table):
+    length = table.shape[1] // 2
+    mul = partial(jnp.dot, preferred_element_type=F32)
+    both = mul(pair[0], table[...])
+    return both[:, :length] + (both[:, length:] + mul(pair[1], table[:, :length]))
+
+
 def plane_kernel(
     bands,
     cols_ref,
     field_ref,
     weight_ref,
-    up_hi,
-    up_lo,
-    down_hi,
-    down_lo,
+    up,
+    down,
     column_hi,
     column_lo,
     back_hi,
     back_lo,
-    grid,
+    out_ref,
     flat,
     sticks,
+    grid,
+    other,
 ):
     devices, part_rows, block = field_ref.shape
     planes = part_rows // 2
     own = block // bands
-    pairs = own // 2
     length = weight_ref.shape[1]
     bz = bands * planes
     slots = LANES // (2 * bz)
     inner = length // slots
     group_rows = inner * length
-    batch = math.gcd(inner, 4)
+    batch = math.gcd(inner, 8)
     total = devices * own
     shift = group_rows.bit_length() - 1
 
@@ -223,19 +234,14 @@
 
     lane = lax.broadcasted_iota(jnp.int32, (1, LANES), 1)
     slot_of_lane = lane // bz % slots
-    chunks = pairs // GROUP
-
-    @pl.loop(0, devices * chunks)
+
+    @pl.loop(0, total // GROUP)
     def _(step):
-        device = lax.div(step, chunks)
-        start = (step - device * chunks) * GROUP
-        first = device * own + 2 * start
-        cols = [cols_ref[first + i] for i in range(2 * GROUP)]
+        base = pl.multiple_of(step * GROUP, GROUP)
+        cols = [cols_ref[base + i] for i in range(GROUP)]
         rows = [col & (group_rows - 1) for col in cols]
         masks = [slot_of_lane == lax.shift_right_logical(col, shift) for col in cols]
-        base = pl.multiple_of(device * own + start, GROUP)
-        places = [base + (i % 2) * pairs + i // 2 for i in range(2 * GROUP)]
-        values = [sticks[pl.ds(place, 1), :] for place in places]
+        values = [sticks[pl.ds(base + i, 1), :] for i in range(GROUP)]
         for value, row, mask in zip(values, rows, masks):
             pltpu.store(grid.at[pl.ds(row, 1), :], value, mask=mask)
 
@@ -249,11 +255,11 @@
             his.append(jnp.concatenate([hi, turn(hi)], axis=1))
             los.append(jnp.concatenate([lo, turn(lo)], axis=1))
         pair = (jnp.concatenate(his, axis=0), jnp.concatenate(los, axis=0))
-        grid[whole, :] = dot3(pair, (up_hi[...], up_lo[...]))
+        other[whole, :] = row_product(pair, up)
 
     for z in range(planes):
         picks = [pl.ds(band * planes + z, 2 * length, stride=bz) for band in range(bands)]
-        value = jnp.concatenate([grid[pick, :] for pick in picks], axis=1)
+        value = jnp.concatenate([other[pick, :] for pick in picks], axis=1)
         value = dot3((column_hi[...], column_lo[...]), split(value))
         weight = weight_ref[pl.ds(z, length, stride=planes), :]
         weight = jnp.concatenate([weight] * 2, axis=0)
@@ -271,13 +277,14 @@
             his.append(jnp.concatenate([hi, turn(hi)], axis=1))
             los.append(jnp.concatenate([lo, turn(lo)], axis=1))
         pair = (jnp.concatenate(his, axis=0), jnp.concatenate(los, axis=0))
-        value = dot3(pair, (down_hi[...], down_lo[...]))
+        value = row_product(pair, down)
         for i, start in enumerate(starts):
-            grid[pl.ds(start, length), :] = value[i * length : (i + 1) * length].T
+            out_ref[pl.ds(start, length), :] = value[i * length : (i + 1) * length].T
 
 
 def depth_down(
     cols_ref,
+    slot_ref,
     grid_ref,
     pw_ref,
     table_hi,
@@ -287,6 +294,7 @@
     field,
     sticks,
     flat,
+    column,
     sent,
     got,
 ):
@@ -302,32 +310,31 @@
     half = slots * bz
     group_rows = grid_ref.shape[0]
     shift = group_rows.bit_length() - 1
-    lane = lax.broadcasted_iota(jnp.int32, (1, LANES), 1)
-    slot_of_lane = lane // bz % slots
+    group = math.gcd(own, GROUP)
 
     def gather(device):
-        @pl.loop(0, rows // GROUP)
+        @pl.loop(0, own // group)
         def _(chunk):
-            start = pl.multiple_of(chunk * GROUP, GROUP)
-            first = device * own + 2 * start
-            cols = [cols_ref[first + i] for i in range(2 * GROUP)]
-            masks = [slot_of_lane == lax.shift_right_logical(col, shift) for col in cols]
+            start = pl.multiple_of(chunk * group, group)
+            first = device * own + start
+            cols = [cols_ref[first + i] for i in range(group)]
             values = [grid_ref[pl.ds(col & (group_rows - 1), 1), :] for col in cols]
-            for i, (value, mask) in enumerate(zip(values, masks)):
-                sticks[pl.ds(start + (i % 2) * rows + i // 2, 1), :] = jnp.where(
-                    mask, value, 0.0
-                )
+            for i, value in enumerate(values):
+                sticks[pl.ds(start + i, 1), :] = value
+
+        slot_of = lax.shift_right_logical(slot_ref[device], shift)
 
         tiles = []
         for tile in range(sticks.shape[0] // LANES):
             value = sticks[tile * LANES : (tile + 1) * LANES].T
+            here = slot_of[:, tile * LANES : (tile + 1) * LANES]
             sums = []
             for part in range(2):
-                terms = [
-                    value[part * half + slot * bz : part * half + (slot + 1) * bz]
-                    for slot in range(slots)
-                ]
-                sums.append(sum(terms[1:], terms[0]))
+                total = value[part * half : part * half + bz]
+                for slot in range(1, slots):
+                    start = part * half + slot * bz
+                    total = jnp.where(here == slot, value[start : start + bz], total)
+                sums.append(total)
             tiles.append(jnp.concatenate(sums, axis=0))
         value = jnp.concatenate(tiles, axis=1)[:, :own]
         for part in range(2):
@@ -343,7 +350,8 @@
     peers.met()
 
     @pl.loop(1, devices)
-    def _(step):
+    def _(turn):
+        step = peers.step(turn)
         gather(peers.at(step))
         peers.copy(step, ready, field, sent, got).start()
 
@@ -352,13 +360,14 @@
     peers.settle(ready, field, sent, got)
     for device in range(devices):
         flat[device * part_rows : (device + 1) * part_rows] = field[device]
-    column = dot3(split(flat[...]), (table_hi[...], table_lo[...]), ((0,), (0,)))
+    value = dot3(split(flat[...]), (table_hi[...], table_lo[...]), ((0,), (0,)))
+    column[0] = value[:, :length]
+    column[1] = value[:, length:]
     for band in range(bands):
         for part in range(2):
             taken = []
             for parity in range(2):
-                start = (band * 2 + parity) * rows
-                piece = column[start : start + rows, part * length : (part + 1) * length]
+                piece = column[part, pl.ds(band * own + parity, rows, stride=2), :]
                 taken.append(
                     jnp.take_along_axis(piece, pw, axis=1, mode="promise_in_bounds")
                 )
@@ -387,11 +396,12 @@
     coeff = dpsi.reshape(2, bands, pairs, 2 * zpw)
 
     depth = halves(depth_table(length, devices))
-    up, down = [halves(table) for table in row_tables(length)]
+    up, down = [jnp.concatenate(halves(table), axis=1) for table in row_tables(length)]
     column = column_table(length, slots)
     back = halves(np.ascontiguousarray(column.T))
     column = halves(column)
 
+    slot_cols = jnp.pad(stick_cols.reshape(devices, 1, own), ((0, 0), (0, 0), (0, -own % LANES)))
     block = (devices, 2 * planes, bands * own)
     in_slots = length // slots * length
     padded = -(-own // LANES) * LANES
@@ -401,44 +411,50 @@
             jax.ShapeDtypeStruct(block, F32),
             jax.ShapeDtypeStruct((length * planes, length), F32),
         ],
-        in_specs=[VM] * 4 + [pl.BlockSpec(memory_space=pl.ANY)] * 2,
+        in_specs=[VM] * 2 + [pl.BlockSpec(memory_space=pltpu.HBM)] * 4,
         out_specs=[VM, VM],
         scratch_shapes=[
             pltpu.VMEM(block, F32),
+            pltpu.VMEM((2, bands * own, length), F32),
+            pltpu.VMEM(depth[0].shape, BF16),
+            pltpu.VMEM(depth[1].shape, BF16),
             pltpu.VMEM(v_local.shape, F32),
             pltpu.VMEM(v_local.shape, F32),
             pltpu.SemaphoreType.DMA((devices,)),
             pltpu.SemaphoreType.DMA((devices,)),
-            pltpu.SemaphoreType.DMA((2,)),
+            pltpu.SemaphoreType.DMA((4,)),
         ],
         compiler_params=params(collective_id=0, has_side_effects=True),
     )(coeff, rows, *depth, v_local, dv)
     grid = pl.pallas_call(
         partial(plane_kernel, bands),
         out_shape=jax.ShapeDtypeStruct((in_slots, LANES), F32),
-        in_specs=[SM] + [VM] * 10,
+        in_specs=[SM] + [VM] * 8,
         out_specs=VM,
         scratch_shapes=[
             pltpu.VMEM((2 * bz, devices * own), F32),
             pltpu.VMEM((devices * own, LANES), F32),
+            pltpu.VMEM((in_slots, LANES), F32),
+            pltpu.VMEM((in_slots, LANES), F32),
         ],
         compiler_params=params(),
-    )(stick_cols, field, potential, *up, *down, *column, *back)
+    )(stick_cols, field, potential, up, down, *column, *back)
     output = pl.pallas_call(
         depth_down,
         out_shape=jax.ShapeDtypeStruct(coeff.shape, F32),
-        in_specs=[SM] + [VM] * 4,
+        in_specs=[SM] + [VM] * 5,
         out_specs=VM,
         scratch_shapes=[
             pltpu.VMEM(block, F32),
             pltpu.VMEM(block, F32),
             pltpu.VMEM((padded, LANES), F32),
             pltpu.VMEM((2 * length, bands * own), F32),
+            pltpu.VMEM((2, bands * own, length), F32),
             pltpu.SemaphoreType.DMA((devices,)),
             pltpu.SemaphoreType.DMA((devices,)),
         ],
         compiler_params=params(collective_id=1, has_side_effects=True),
-    )(stick_cols, grid, rows, *depth)
+    )(stick_cols, slot_cols, grid, rows, *depth)
     return output.reshape(dpsi.shape)
 
 

time: 56.3 us -> 51.8 us (0.920)
  Pallas kernels: 48.5 us -> 44 us
    pallas_call x1, Pallas kernels: 17.3 us -> 12.4 us  [local(): pl.pallas_call(partial(plane_kernel, bands), out_shape=jax.ShapeDtypeStru...]
    pallas_call x1, Pallas kernels: 14 us -> 16.9 us  [local(): pl.pallas_call(depth_up, out_shape=[jax.ShapeDtypeStruct(block, F32), jax...]
    pallas_call x1, Pallas kernels: 17.2 us -> 14.6 us  [local(): pl.pallas_call(depth_down, out_shape=jax.ShapeDtypeStruct(coeff.shape, F3...]
    unnamed x32 -> x28, local copies, waits for them, and re-layouts: 5.12 us -> 5.13 us
where the time goes in v1:
time: 51.8 us; the launch traced here: 51.5 us
  Pallas kernels  44 us (85%)
  local copies, waits for them, and re-layouts  7.38 us (14%)
    pallas_call x1, Pallas kernels, local(): pl.pallas_call(depth_up, out_shape=[jax.ShapeDtypeStruct(block, F32), jax...  16.9 us
    pallas_call x1, Pallas kernels, local(): pl.pallas_call(depth_down, out_shape=jax.ShapeDtypeStruct(coeff.shape, F3...  14.6 us
    pallas_call x1, Pallas kernels, local(): pl.pallas_call(partial(plane_kernel, bands), out_shape=jax.ShapeDtypeStru...  12.4 us
    unnamed x28, local copies, waits for them, and re-layouts  5.13 us
    reshape x1, local copies, waits for them, and re-layouts, local(): coeff = dpsi.reshape(2, bands, pairs, 2 * zpw)  1.1 us

profile of v1, /device:TPU:0, one launch (start us, length us, event | category | flops | bytes accessed | tf_op | source)
XLA Modules:
  0.0 51.5 jit_solution(15165465847014208782)
XLA Ops:
  0.0 0.0 copy-start.10
  0.0 0.0 copy-start.11
  0.0 0.0 copy-start.12
  0.1 0.8 %copy-done = s32[384,64]{0,1:T(8,128)S(1)} copy-done((s32[384,64]{0,1:T(8,128)S(1)}, s32[384,64]{0,1:T(8,128)}, u32[]{:S(2)}) %copy-start) | copy-done | bytes 98328
  0.9 0.1 constant_dynamic-slice_fusion
  1.0 0.1 copy.17
  1.1 0.1 reshape.14.pw_ref
  1.2 1.1 %reshape.13.coeff_ref = f32[2,2,96,128]{3,2,1,0:T(8,128)S(1)} reshape(f32[2,2,12288]{2,1,0:T(2,128)} %param.15) | data formatting | bytes 393216 | tf_op jit(solution)/shard_map/reshape | solution.py:396
  2.3 0.0 copy-start.1
  2.3 1.2 %copy-done.1 = f32[16,16384]{1,0:T(8,128)S(1)} copy-done((f32[16,16384]{1,0:T(8,128)S(1)}, f32[16,16384]{1,0:T(8,128)}, u32[]{:S(2)}) %copy-start.1) | copy-done | bytes 1048600
  3.5 1.2 %copy-done.2 = f32[16,16384]{1,0:T(8,128)S(1)} copy-done((f32[16,16384]{1,0:T(8,128)S(1)}, f32[16,16384]{1,0:T(8,128)}, u32[]{:S(2)}) %copy-start.2) | copy-done | bytes 1048600
  4.7 0.9 %copy-done.3 = bf16[256,256]{1,0:T(8,128)(2,1)S(1)} copy-done((bf16[256,256]{1,0:T(8,128)(2,1)S(1)}, bf16[256,256]{1,0:T(8,128)(2,1)}, u32[]{:S(2)}) %copy-start.3) | copy-done | bytes 131096
  5.6 0.9 %copy-done.5 = bf16[256,256]{1,0:T(8,128)(2,1)S(1)} copy-done((bf16[256,256]{1,0:T(8,128)(2,1)S(1)}, bf16[256,256]{1,0:T(8,128)(2,1)}, u32[]{:S(2)}) %copy-start.5) | copy-done | bytes 131096
  6.5 16.9 %shard_map.145 = (f32[16,16,384]{2,1,0:T(8,128)S(1)}, f32[1024,128]{1,0:T(8,128)S(1)}) custom-call(f32[2,2,96,128]{3,2,1,0:T(8,128)S(1)} %reshape.13.coeff_ref, s32[96,128]{1,0:T(8,128)S(1)} %reshape.14.pw_ref, bf16[256,256]{1,0:T(8,128)(2,1)S(1)} %copy-done.3, bf16[256,256]{1,0:T(8,128)(2,1)S(1)} %copy-done.5, f32[16,16384]{1,0:T(8,128)S(1)} %copy-done.1, ...), custom_call_target="tpu_custom_call" | custom-call | tf_op jit(solution)/shard_map/pallas_call | solution.py:408
  23.4 0.0 copy-start.4
  23.4 0.0 copy-start.6
  23.4 0.0 copy-done.7
  23.5 0.0 copy-done.8
  23.5 0.0 copy-done.9
  23.5 0.0 copy-done.10
  23.5 12.4 %shard_map.146.grid_ref = f32[4096,128]{1,0:T(8,128)S(1)} custom-call(s32[3072]{0:T(1024)S(1)} %copy-done.13, f32[16,16,384]{2,1,0:T(8,128)S(1)} %get-tuple-element.7.field_ref, f32[1024,128]{1,0:T(8,128)S(1)} %get-tuple-element.8.weight_ref, bf16[256,256]{1,0:T(8,128)(2,1)S(1)} %copy-done.11, bf16[256,256]{1,0:T(8,128)(2,1)S(1)} %copy-done.12, ...), custom_call_target="tpu_custom_call" | custom-call | tf_op jit(solution)/shard_map/pallas_call | solution.py:429
  35.9 0.1 reshape.12
  36.1 14.6 %shard_map.147 = f32[2,2,96,128]{3,2,1,0:T(8,128)S(1)} custom-call(s32[3072]{0:T(1024)S(1)} %copy-done.13, s32[16,1,256]{2,1,0:T(1,128)S(1)} %pad.4.slot_ref, f32[4096,128]{1,0:T(8,128)S(1)} %shard_map.146.grid_ref, s32[96,128]{1,0:T(8,128)S(1)} %reshape.14.pw_ref, bf16[256,256]{1,0:T(8,128)(2,1)S(1)} %copy-done.4, bf16[256,256]{1,0:T(8,128)(2,1)S(1)} %copy-done.6), custom_call_target="tpu_custom_call" | custom-call | tf_op jit(solution)/shard_map/pallas_call | solution.py:442
  50.7 0.8 %reshape.15 = f32[2,2,12288]{2,1,0:T(2,128)} reshape(f32[2,2,96,128]{3,2,1,0:T(8,128)S(1)} %shard_map.147) | data formatting | bytes 393216 | tf_op jit(solution)/shard_map/reshape | solution.py:458
  (14 shorter events, 0.0 us)
Async XLA Ops:
  0.0 0.9 %copy-start = (s32[384,64]{0,1:T(8,128)S(1)}, s32[384,64]{0,1:T(8,128)}, u32[]{:S(2)}) copy-start(s32[384,64]{0,1:T(8,128)} %param.17) | copy-start | bytes 294916
  0.0 23.4 %copy-start.7 = (bf16[256,256]{1,0:T(8,128)(2,1)S(1)}, bf16[256,256]{1,0:T(8,128)(2,1)}, u32[]{:S(2)}) copy-start(bf16[256,256]{1,0:T(8,128)(2,1)} %constant.36.clone.back_hi) | copy-start | bytes 393220
  0.0 23.4 %copy-start.8 = (bf16[256,256]{1,0:T(8,128)(2,1)S(1)}, bf16[256,256]{1,0:T(8,128)(2,1)}, u32[]{:S(2)}) copy-start(bf16[256,256]{1,0:T(8,128)(2,1)} %constant.37.clone.back_lo) | copy-start | bytes 393220
  0.0 23.5 %copy-start.9 = (bf16[256,256]{1,0:T(8,128)(2,1)S(1)}, bf16[256,256]{1,0:T(8,128)(2,1)}, u32[]{:S(2)}) copy-start(bf16[256,256]{1,0:T(8,128)(2,1)} %constant.38.clone.column_hi) | copy-start | bytes 393220
  0.0 23.5 %copy-start.10 = (bf16[256,256]{1,0:T(8,128)(2,1)S(1)}, bf16[256,256]{1,0:T(8,128)(2,1)}, u32[]{:S(2)}) copy-start(bf16[256,256]{1,0:T(8,128)(2,1)} %constant.39.clone.column_lo) | copy-start | bytes 393220
  0.0 23.5 %copy-start.11 = (bf16[256,256]{1,0:T(8,128)(2,1)S(1)}, bf16[256,256]{1,0:T(8,128)(2,1)}, u32[]{:S(2)}) copy-start(bf16[256,256]{1,0:T(8,128)(2,1)} %constant.42.up) | copy-start | bytes 393220
  0.0 23.5 %copy-start.12 = (bf16[256,256]{1,0:T(8,128)(2,1)S(1)}, bf16[256,256]{1,0:T(8,128)(2,1)}, u32[]{:S(2)}) copy-start(bf16[256,256]{1,0:T(8,128)(2,1)} %constant.43.down) | copy-start | bytes 393220
  0.1 23.5 %copy-start.13 = (s32[3072]{0:T(1024)S(1)}, s32[3072]{0:T(1024)}, u32[]{:S(2)}) copy-start(s32[3072]{0:T(1024)} %cols_ref.3) | copy-start | bytes 36868
  2.3 1.2 %copy-start.1 = (f32[16,16384]{1,0:T(8,128)S(1)}, f32[16,16384]{1,0:T(8,128)}, u32[]{:S(2)}) copy-start(f32[16,16384]{1,0:T(8,128)} %local_ref.1) | copy-start | bytes 3145732
  3.5 1.2 %copy-start.2 = (f32[16,16384]{1,0:T(8,128)S(1)}, f32[16,16384]{1,0:T(8,128)}, u32[]{:S(2)}) copy-start(f32[16,16384]{1,0:T(8,128)} %change_ref.1) | copy-start | bytes 3145732
  4.7 0.9 %copy-start.3 = (bf16[256,256]{1,0:T(8,128)(2,1)S(1)}, bf16[256,256]{1,0:T(8,128)(2,1)}, u32[]{:S(2)}) copy-start(bf16[256,256]{1,0:T(8,128)(2,1)} %constant.30.clone.hi_ref.table_hi) | copy-start | bytes 393220
  5.6 0.9 %copy-start.5 = (bf16[256,256]{1,0:T(8,128)(2,1)S(1)}, bf16[256,256]{1,0:T(8,128)(2,1)}, u32[]{:S(2)}) copy-start(bf16[256,256]{1,0:T(8,128)(2,1)} %constant.31.clone.lo_ref.table_lo) | copy-start | bytes 393220
  23.4 12.6 %copy-start.4 = (bf16[256,256]{1,0:T(8,128)(2,1)S(1)}, bf16[256,256]{1,0:T(8,128)(2,1)}, u32[]{:S(2)}) copy-start(bf16[256,256]{1,0:T(8,128)(2,1)} %constant.30.clone.hi_ref.table_hi) | copy-start | bytes 393220
  23.4 12.6 %copy-start.6 = (bf16[256,256]{1,0:T(8,128)(2,1)S(1)}, bf16[256,256]{1,0:T(8,128)(2,1)}, u32[]{:S(2)}) copy-start(bf16[256,256]{1,0:T(8,128)(2,1)} %constant.31.clone.lo_ref.table_lo) | copy-start | bytes 393220
